TPU v7x, 32 devices: a whole 2x2x4 slice. The times are simulated.
32 devices in a mesh: grp: 8 (over y, x, core), chan: 4 (over z).
Axes of the slice: x: 2, y: 2, z: 4, core: 2. Of those that a mesh axis runs over, the one named last changes fastest.
Arguments:
- spectra: bfloat16 [512, 2, 2, 8192], P(('grp', 'chan')), may hold values from -45 to 45
- pair_blocks: int32 [8, 4, 18, 2], P('grp', 'chan'), may hold values from 0 to 31
- owners: int32 [8, 4, 18, 1], P('grp', 'chan'), may hold values from 0 to 7; in each aligned block of 18 rows (0 to 17, 18 to 35, ..., all dimensions but the last counted through in order) at most 3 rows name the same one
Outputs:
- stacks: float32 [8, 4, 24, 4, 1024], P('grp', 'chan')
Inputs may be any that keep to these rules, and one draw needn't show every extreme that they name: `owners`: at most 3 of one device's 18 pair blocks name the same owner.
All inputs are finite; a program needn't handle non-finite values.
Results may differ from a plain program's by a relative error of at most 0.011.
Values may be sent and summed in bfloat16 or wider, within the bound.
No kernel may reach another device: no remote copies, remote signals or barrier semaphores. Data moves between devices by JAX's collectives and lax.ppermute only.
A program may use at most 128 MiB of HBM per device.

v0:
```python
import functools

import jax
import jax.numpy as jnp
from jax import lax
from jax.experimental import pallas as pl
from jax.experimental.pallas import tpu as pltpu
from jax.sharding import PartitionSpec as P

F = 8192
LAGS = 1024
BLK = 2
NB_SRC = 18
MOST = 3
WINDOWS = 2
LANES = 128
PAIRS = BLK * BLK
VMEM_LIMIT = 48 * 1024 * 1024


def whiten_kernel(parts, spec_ref, notes_ref, out_ref):
    blocks = F // LANES
    each = blocks // parts

    def values(k):
        span = slice(k * LANES, (k + 1) * LANES)
        re = spec_ref[0, :, span].astype(jnp.float32)
        im = spec_ref[1, :, span].astype(jnp.float32)
        return re, im, re * re + im * im

    for z in range(parts):
        out_ref[z, :, each * 2 * LANES :] = notes_ref[...]
    sums = [None] * 4
    for k in range(blocks):
        power = values(k)[2]
        sums[k % 4] = power if k < 4 else sums[k % 4] + power
    total = jnp.sum((sums[0] + sums[1]) + (sums[2] + sums[3]), axis=1, keepdims=True)
    level = 0.1 * (total * (1.0 / F) + 1e-05)
    for k in range(blocks):
        re, im, power = values(k)
        scale = lax.rsqrt(power + level)
        at = k % each * 2 * LANES
        out_ref[k // each, :, at : at + LANES] = (re * scale).astype(jnp.bfloat16)
        out_ref[k // each, :, at + LANES : at + 2 * LANES] = (im * scale).astype(jnp.bfloat16)


def whiten(spectra, notes, parts):
    rows = spectra.shape[0] * WINDOWS
    step = 16
    planes = jnp.transpose(spectra.reshape(rows, 2, F), (1, 0, 2))
    width = 2 * F // parts + LANES
    return pl.pallas_call(
        functools.partial(whiten_kernel, parts),
        grid=(rows // step,),
        in_specs=[
            pl.BlockSpec((2, step, F), lambda i: (0, i, 0)),
            pl.BlockSpec((step, LANES), lambda i: (i, 0)),
        ],
        out_specs=pl.BlockSpec((parts, step, width), lambda i: (0, i, 0)),
        out_shape=jax.ShapeDtypeStruct((parts, rows, width), jnp.bfloat16),
        name="whiten",
    )(planes, notes)


def table_kernel(first_ref, hi_cos_ref, hi_sin_ref, lo_cos_ref, lo_sin_ref, out_ref):
    s = pl.program_id(0)
    hi_cos = hi_cos_ref[pl.ds(s, 1), :]
    hi_sin = hi_sin_ref[pl.ds(s, 1), :]
    lo_cos = lo_cos_ref[...]
    lo_sin = lo_sin_ref[...]
    zero_bin = jnp.logical_and(first_ref[0] == 0, s == 0)
    row = lax.broadcasted_iota(jnp.int32, lo_cos.shape, 0)
    weight = jnp.where(jnp.logical_and(row == 0, zero_bin), 0.5, 1.0)
    out_ref[0:LANES] = ((hi_cos * lo_cos - hi_sin * lo_sin) * weight).astype(jnp.bfloat16)
    out_ref[LANES:] = -((hi_sin * lo_cos + hi_cos * lo_sin) * weight).astype(jnp.bfloat16)


def tables(place, chunks):
    lag = jnp.arange(LAGS, dtype=jnp.int32) - LAGS // 2

    def angles(bins):
        phase = bins[:, None] * lag[None, :] % (2 * F)
        return phase.astype(jnp.float32) * (jnp.pi / F)

    high = angles((place * chunks + jnp.arange(chunks, dtype=jnp.int32)) * LANES)
    low = angles(jnp.arange(LANES, dtype=jnp.int32))
    unit = 2.0 / jnp.sqrt(jnp.float32(F))
    whole = lambda shape: pl.BlockSpec(shape, lambda s, first: (0, 0))
    return pl.pallas_call(
        table_kernel,
        grid_spec=pltpu.PrefetchScalarGridSpec(
            num_scalar_prefetch=1,
            grid=(chunks,),
            in_specs=[
                whole((chunks, LAGS)),
                whole((chunks, LAGS)),
                whole((LANES, LAGS)),
                whole((LANES, LAGS)),
            ],
            out_specs=pl.BlockSpec((2 * LANES, LAGS), lambda s, first: (s, 0)),
        ),
        out_shape=jax.ShapeDtypeStruct((chunks * 2 * LANES, LAGS), jnp.bfloat16),
        cost_estimate=pl.CostEstimate(
            flops=chunks * LANES * LAGS * 8, bytes_accessed=chunks * LANES * LAGS * 4, transcendentals=0
        ),
        name="tables",
    )(place[None], jnp.cos(high) * unit, jnp.sin(high) * unit, jnp.cos(low), jnp.sin(low))


def choosers(parts, notes_ref, rows_ref, place_ref):
    count = parts * NB_SRC
    height = notes_ref.shape[0]

    def iota(shape, axis):
        return lax.broadcasted_iota(jnp.int32, shape, axis).astype(jnp.float32)

    line = iota((count, height), 0)
    at = line
    for z in range(1, parts):
        at = at + jnp.where(line >= z * NB_SRC, float(height // parts - NB_SRC), 0.0)
    listed = (at == iota((count, height), 1)).astype(jnp.float32).astype(jnp.bfloat16)
    notes = jnp.dot(listed, notes_ref[...], preferred_element_type=jnp.float32)
    left, right, owner, source = [notes[:, i : i + 1] for i in range(4)]
    across = iota((count, height), 1)
    picks = []
    for block in (left, right):
        for offset in range(BLK * WINDOWS):
            hit = across == block * (BLK * WINDOWS) + offset
            picks.append(hit.astype(jnp.float32))
    rows_ref[...] = jnp.concatenate(picks, axis=0).astype(jnp.bfloat16)

    owned = (iota((count, LANES), 1) == owner).astype(jnp.float32)
    other = iota((count, count), 1)
    before = jnp.logical_and(other < iota((count, count), 0), other >= source * NB_SRC)
    before = before.astype(jnp.float32).astype(jnp.bfloat16)
    seen = jnp.dot(before, owned.astype(jnp.bfloat16), preferred_element_type=jnp.float32)
    rank = jnp.sum(owned * seen, axis=1, keepdims=True)
    target = ((owner * parts + source) * MOST + rank) * PAIRS
    across = iota((count, place_ref.shape[1]), 1)
    places = [(across == target + n).astype(jnp.float32) for n in range(PAIRS)]
    place_ref[...] = jnp.concatenate(places, axis=0).astype(jnp.bfloat16)


def corr_kernel(per_step, parts, notes_ref, panel_ref, table_ref, out_ref, total, rows_ref, place_ref):
    step = pl.program_id(0)
    count = total.shape[0] // PAIRS

    @pl.when(step == 0)
    def prepare():
        choosers(parts, notes_ref, rows_ref, place_ref)

    chosen = jnp.dot(rows_ref[...], panel_ref[...], preferred_element_type=jnp.float32)

    def row(side, channel, window, start):
        first = ((side * BLK + channel) * WINDOWS + window) * count
        return chosen[first : first + count, start : start + LANES]

    columns = []
    for i in range(per_step):
        at = i * 2 * LANES
        real = []
        imag = []
        for p in range(BLK):
            for q in range(BLK):
                re = 0.0
                im = 0.0
                for w in range(WINDOWS):
                    ra, ia = row(0, p, w, at), row(0, p, w, at + LANES)
                    rb, ib = row(1, q, w, at), row(1, q, w, at + LANES)
                    re = re + (ra * rb + ia * ib)
                    im = im + (ia * rb - ra * ib)
                real.append(re * (1.0 / WINDOWS))
                imag.append(im * (1.0 / WINDOWS))
        columns.append(jnp.concatenate(real, axis=0).astype(jnp.bfloat16))
        columns.append(jnp.concatenate(imag, axis=0).astype(jnp.bfloat16))
    part = jnp.dot(
        jnp.concatenate(columns, axis=1), table_ref[...], preferred_element_type=jnp.float32
    )

    @pl.when(step == 0)
    def start():
        total[...] = part

    @pl.when(step > 0)
    def add():
        total[...] += part

    @pl.when(step == pl.num_programs(0) - 1)
    def finish():
        out_ref[...] = lax.dot_general(
            place_ref[...],
            total[...].astype(jnp.bfloat16),
            (((0,), (0,)), ((), ())),
            preferred_element_type=jnp.float32,
        ).astype(jnp.bfloat16)


def correlate(panel, table, groups, parts):
    per_step = 4
    span = per_step * 2 * LANES
    height = panel.shape[0]
    steps = panel.shape[1] // span
    pairs = parts * NB_SRC * PAIRS
    slots = groups * parts * MOST * PAIRS
    return pl.pallas_call(
        functools.partial(corr_kernel, per_step, parts),
        grid=(steps,),
        in_specs=[
            pl.BlockSpec((height, LANES), lambda i: (0, steps * span // LANES)),
            pl.BlockSpec((height, span), lambda i: (0, i)),
            pl.BlockSpec((span, LAGS), lambda i: (i, 0)),
        ],
        out_specs=pl.BlockSpec((slots, LAGS), lambda i: (0, 0)),
        scratch_shapes=[
            pltpu.VMEM((pairs, LAGS), jnp.float32),
            pltpu.VMEM((2 * pairs, height), jnp.bfloat16),
            pltpu.VMEM((pairs, slots), jnp.bfloat16),
        ],
        out_shape=jax.ShapeDtypeStruct((slots, LAGS), jnp.bfloat16),
        compiler_params=pltpu.CompilerParams(vmem_limit_bytes=VMEM_LIMIT),
        cost_estimate=pl.CostEstimate(
            flops=2 * pairs * steps * span * LAGS,
            bytes_accessed=steps * span * LAGS * 2,
            transcendentals=0,
        ),
        name="correlate",
    )(panel, panel, table)


def local(spectra, pair_blocks, owners):
    groups = lax.axis_size("grp")
    parts = lax.axis_size("chan")
    place = lax.axis_index("chan")
    chunks = F // LANES // parts
    rows = spectra.shape[0] * WINDOWS

    lane = lax.broadcasted_iota(jnp.int32, (NB_SRC, LANES), 1)
    blocks = pair_blocks[0, 0]
    notes = jnp.where(lane == 0, blocks[:, :1], jnp.where(lane == 1, blocks[:, 1:], place))
    notes = jnp.where(lane == 2, owners[0, 0], notes).astype(jnp.bfloat16)
    notes = jnp.pad(notes, ((0, rows - NB_SRC), (0, 0)))
    white = whiten(spectra, notes, parts)
    panel = lax.all_to_all(white, "chan", split_axis=0, concat_axis=0, tiled=True)
    panel = panel.reshape(parts * rows, white.shape[2])

    table = tables(place, chunks)
    corr = correlate(panel, table, groups, parts)
    corr = corr.reshape(groups * parts, MOST, PAIRS, LAGS)
    got = lax.all_to_all(corr, ("grp", "chan"), split_axis=0, concat_axis=0, tiled=True)
    got = got.reshape(groups, parts, MOST, PAIRS, LAGS).astype(jnp.float32)
    return jnp.sum(got, axis=1).reshape(1, 1, groups * MOST, PAIRS, LAGS)


def solution(mesh):
    return jax.shard_map(
        local,
        mesh=mesh,
        in_specs=(
            P(("grp", "chan"), None, None, None),
            P("grp", "chan", None, None),
            P("grp", "chan", None, None),
        ),
        out_specs=P("grp", "chan", None, None, None),
        check_vma=False,
    )
```

profile of v0, /device:TPU:0, one launch (start us, length us, event | category | flops | bytes accessed | tf_op | source)
XLA Modules:
  0.0 72.6 jit_solution(7797927818911138788)
XLA Ops:
  0.0 0.0 copy-start
  0.0 0.8 %slice_bitcast_fusion.1 = (s32[18]{0:T(128)S(1)}, s32[18]{0:T(128)S(1)}) fusion(s32[18,2]{0,1:T(2,128)} %bitcast.20), kind=kLoop, calls=%fused_computation.28 | loop fusion | bytes 288 | tf_op jit(solution)/shard_map/jit(_where)/broadcast_in_dim | solution.py:239
  0.8 2.8 %copy.7 = bf16[32,2,8192]{2,0,1:T(8,128)(2,1)} copy(bf16[32,2,8192]{2,1,0:T(2,128)(2,1)} %bitcast.19) | data formatting | bytes 2097152 | tf_op jit(solution)/shard_map/reshape | solution.py:50
  3.5 0.0 copy-done
  3.6 0.1 select_convert_fusion
  3.6 0.6 pad.4.notes_ref
  4.2 2.5 %whiten.1 = bf16[4,32,4224]{2,1,0:T(8,128)(2,1)} custom-call(bf16[2,32,8192]{2,1,0:T(8,128)(2,1)} %bitcast.18, bf16[32,128]{1,0:T(8,128)(2,1)} %pad.4.notes_ref), custom_call_target="tpu_custom_call" | custom-call | tf_op jit(solution)/shard_map/whiten/pallas_call | solution.py:52
  6.8 6.3 %all-to-all-start = ((bf16[4,32,4224]{2,1,0:T(8,128)(2,1)}), bf16[4,32,4224]{2,1,0:T(8,128)(2,1)S(1)}, u32[]{:S(2)}, u32[]{:S(2)}) async-start(bf16[4,32,4224]{2,1,0:T(8,128)(2,1)} %whiten.1), calls=%async_computation | async-start | bytes 2162688 | tf_op jit(solution)/shard_map/all_to_all | solution.py:243
  13.1 1.0 %sine_multiply_fusion = (f32[16,1024]{1,0:T(8,128)}, f32[16,1024]{1,0:T(8,128)}) fusion(s32[1024]{0:T(1024)S(1)} %iota_add_fusion, s32[16]{0:T(128)S(1)} %add_multiply_fusion), kind=kLoop, calls=%fused_computation.21 | loop fusion | flops 262144 | bytes 135232 | tf_op jit(solution)/shard_map/mul | solution.py:107
  14.1 2.9 %fusion.6 = (f32[128,1024]{1,0:T(8,128)}, f32[128,1024]{1,0:T(8,128)}) fusion(s32[1024]{0:T(1024)S(1)} %iota_add_fusion), kind=kLoop, calls=%fused_computation.11 | loop fusion | flops 1835008 | bytes 1052672 | tf_op jit(solution)/shard_map/sin | solution.py:107
  17.0 9.2 %tables.1.table_ref = bf16[4096,1024]{1,0:T(8,128)(2,1)} custom-call(s32[1]{0:T(128)} %bitcast.7.first_ref, f32[16,1024]{1,0:T(8,128)} %get-tuple-element.6.hi_cos_ref, f32[16,1024]{1,0:T(8,128)} %get-tuple-element.5.hi_sin_ref, f32[128,1024]{1,0:T(8,128)} %get-tuple-element.8.lo_cos_ref, f32[128,1024]{1,0:T(8,128)} %get-tuple-element.7.lo_sin_ref), custom_call_target="tpu_custom_call" | custom-call | flops 16777216 | bytes 8388608 | tf_op jit(solution)/shard_map/tables/pallas_call | solution.py:89
  26.2 13.3 %all-to-all-done = bf16[4,32,4224]{2,1,0:T(8,128)(2,1)S(1)} async-done(((bf16[4,32,4224]{2,1,0:T(8,128)(2,1)}), bf16[4,32,4224]{2,1,0:T(8,128)(2,1)S(1)}, u32[]{:S(2)}, u32[]{:S(2)}) %all-to-all-start) | async-done | bytes 1081376 | tf_op jit(solution)/shard_map/all_to_all | solution.py:243
  39.5 8.6 %correlate.1 = bf16[384,1024]{1,0:T(8,128)(2,1)S(1)} custom-call(bf16[128,4224]{1,0:T(8,128)(2,1)S(1)} %bitcast.16, bf16[128,4224]{1,0:T(8,128)(2,1)S(1)} %bitcast.17, bf16[4096,1024]{1,0:T(8,128)(2,1)} %tables.1.table_ref), custom_call_target="tpu_custom_call" | custom-call | flops 2415919104 | bytes 8388608 | tf_op jit(solution)/shard_map/correlate/pallas_call | solution.py:205
  48.1 0.3 reshape.27
  48.4 23.1 %all_to_all.10 = bf16[32,3,4,1024]{3,2,1,0:T(4,128)(2,1)S(1)} all-to-all(bf16[32,3,4,1024]{3,2,1,0:T(4,128)(2,1)S(1)} %reshape.27), channel_id=1, replica_groups=mesh['grp'=8,'chan'=4] {'grp','chan'}, dimensions={0} | all-to-all | bytes 1572864 | tf_op jit(solution)/shard_map/all_to_all | solution.py:249
  71.5 1.1 %convert_reduce_fusion = f32[8,3,4,1024]{3,2,1,0:T(4,128)} fusion(bf16[32,3,4,1024]{3,2,1,0:T(4,128)(2,1)S(1)} %all_to_all.10), kind=kLoop, calls=%fused_computation | loop fusion | flops 688128 | bytes 1179648 | tf_op jit(solution)/shard_map/reduce_sum | solution.py:251
  (4 shorter events, 0.0 us)
Async XLA Ops:
  0.0 3.5 %copy-start = (s32[1,1,18,1]{2,3,1,0:T(1,128)S(1)}, s32[1,1,18,1]{2,3,1,0:T(1,128)}, u32[]{:S(2)}) copy-start(s32[1,1,18,1]{2,3,1,0:T(1,128)} %param.5) | copy-start | bytes 220
  6.8 32.8 %all-to-all-start = ((bf16[4,32,4224]{2,1,0:T(8,128)(2,1)}), bf16[4,32,4224]{2,1,0:T(8,128)(2,1)S(1)}, u32[]{:S(2)}, u32[]{:S(2)}) async-start(bf16[4,32,4224]{2,1,0:T(8,128)(2,1)} %whiten.1), calls=%async_computation | async-start | bytes 2162688 | tf_op jit(solution)/shard_map/all_to_all | solution.py:243
where the time goes:
time: 74 us; the launch traced here: 72.6 us
  blocking collectives  23.1 us (31%)
  Pallas kernels  20.3 us (27%)
  waiting for transfers between devices  13.3 us (18%)
  starting transfers between devices  6.33 us (9%)
  other arithmetic  5.11 us (7%)
  local copies, waits for them, and re-layouts  4.43 us (6%)
    all_to_all x1, blocking collectives, local(): lax.all_to_all(corr, ('grp', 'chan'), split_axis=0, concat_axis=0, tiled=...  23.1 us
    all_to_all x1, waiting for transfers between devices, local(): lax.all_to_all(white, 'chan', split_axis=0, concat_axis=0, tiled=True)  13.3 us
    pallas_call x1, Pallas kernels, tables(): pl.pallas_call(table_kernel, grid_spec=pltpu.PrefetchScalarGridSpec(num_s...  9.22 us
    pallas_call x1, Pallas kernels, correlate(): pl.pallas_call(functools.partial(corr_kernel, per_step, parts), grid=(ste...  8.58 us
    all_to_all x1, starting transfers between devices, local(): lax.all_to_all(white, 'chan', split_axis=0, concat_axis=0, tiled=True)  6.33 us
    sin x1, other arithmetic, tables(): jnp.sin(low)  2.91 us
    reshape x1, local copies, waits for them, and re-layouts, whiten(): planes = jnp.transpose(spectra.reshape(rows, 2, F), (1, 0, 2))  2.77 us
    pallas_call x1, Pallas kernels, whiten(): pl.pallas_call(functools.partial(whiten_kernel, parts), grid=(rows // ste...  2.51 us
  transfers between devices with their start and end apart: 1, of which 1 were waited for; matrix products, arithmetic and copies ran while one was open for 5% of the time, Pallas kernels for 13%

commit v1 on v0

--- a/solution.py
+++ b/solution.py
@@ -18,48 +18,54 @@
 VMEM_LIMIT = 48 * 1024 * 1024
 
 
-def whiten_kernel(parts, spec_ref, notes_ref, out_ref):
+def whiten_kernel(parts, place_ref, spec_ref, notes_ref, *out_refs):
     blocks = F // LANES
     each = blocks // parts
-
-    def values(k):
-        span = slice(k * LANES, (k + 1) * LANES)
+    place = place_ref[0]
+
+    def values(start):
+        span = pl.ds(start, LANES)
         re = spec_ref[0, :, span].astype(jnp.float32)
         im = spec_ref[1, :, span].astype(jnp.float32)
         return re, im, re * re + im * im
 
-    for z in range(parts):
-        out_ref[z, :, each * 2 * LANES :] = notes_ref[...]
+    for out_ref in out_refs:
+        out_ref[:, each * 2 * LANES :] = notes_ref[...]
     sums = [None] * 4
     for k in range(blocks):
-        power = values(k)[2]
+        power = values(k * LANES)[2]
         sums[k % 4] = power if k < 4 else sums[k % 4] + power
     total = jnp.sum((sums[0] + sums[1]) + (sums[2] + sums[3]), axis=1, keepdims=True)
     level = 0.1 * (total * (1.0 / F) + 1e-05)
-    for k in range(blocks):
-        re, im, power = values(k)
-        scale = lax.rsqrt(power + level)
-        at = k % each * 2 * LANES
-        out_ref[k // each, :, at : at + LANES] = (re * scale).astype(jnp.bfloat16)
-        out_ref[k // each, :, at + LANES : at + 2 * LANES] = (im * scale).astype(jnp.bfloat16)
-
-
-def whiten(spectra, notes, parts):
+    for d, out_ref in enumerate(out_refs):
+        first = jnp.bitwise_xor(place, d) * each
+        for k in range(each):
+            re, im, power = values(pl.multiple_of((first + k) * LANES, LANES))
+            scale = lax.rsqrt(power + level)
+            at = k * 2 * LANES
+            out_ref[:, at : at + LANES] = (re * scale).astype(jnp.bfloat16)
+            out_ref[:, at + LANES : at + 2 * LANES] = (im * scale).astype(jnp.bfloat16)
+
+
+def whiten(spectra, notes, place, parts):
     rows = spectra.shape[0] * WINDOWS
     step = 16
     planes = jnp.transpose(spectra.reshape(rows, 2, F), (1, 0, 2))
     width = 2 * F // parts + LANES
     return pl.pallas_call(
         functools.partial(whiten_kernel, parts),
-        grid=(rows // step,),
-        in_specs=[
-            pl.BlockSpec((2, step, F), lambda i: (0, i, 0)),
-            pl.BlockSpec((step, LANES), lambda i: (i, 0)),
-        ],
-        out_specs=pl.BlockSpec((parts, step, width), lambda i: (0, i, 0)),
-        out_shape=jax.ShapeDtypeStruct((parts, rows, width), jnp.bfloat16),
+        grid_spec=pltpu.PrefetchScalarGridSpec(
+            num_scalar_prefetch=1,
+            grid=(rows // step,),
+            in_specs=[
+                pl.BlockSpec((2, step, F), lambda i, place: (0, i, 0)),
+                pl.BlockSpec((step, LANES), lambda i, place: (i, 0)),
+            ],
+            out_specs=[pl.BlockSpec((step, width), lambda i, place: (i, 0))] * parts,
+        ),
+        out_shape=[jax.ShapeDtypeStruct((rows, width), jnp.bfloat16)] * parts,
         name="whiten",
-    )(planes, notes)
+    )(place[None], planes, notes)
 
 
 def table_kernel(first_ref, hi_cos_ref, hi_sin_ref, lo_cos_ref, lo_sin_ref, out_ref):
@@ -107,49 +113,55 @@
     )(place[None], jnp.cos(high) * unit, jnp.sin(high) * unit, jnp.cos(low), jnp.sin(low))
 
 
-def choosers(parts, notes_ref, rows_ref, place_ref):
+def choosers(parts, place, packed, rows_ref, place_ref):
     count = parts * NB_SRC
-    height = notes_ref.shape[0]
+    height = packed.shape[0]
+    blocks = height // parts // (BLK * WINDOWS)
 
     def iota(shape, axis):
-        return lax.broadcasted_iota(jnp.int32, shape, axis).astype(jnp.float32)
+        return lax.broadcasted_iota(jnp.int32, shape, axis)
+
+    def ones(hit):
+        return hit.astype(jnp.float32).astype(jnp.bfloat16)
 
     line = iota((count, height), 0)
     at = line
     for z in range(1, parts):
-        at = at + jnp.where(line >= z * NB_SRC, float(height // parts - NB_SRC), 0.0)
-    listed = (at == iota((count, height), 1)).astype(jnp.float32).astype(jnp.bfloat16)
-    notes = jnp.dot(listed, notes_ref[...], preferred_element_type=jnp.float32)
+        at = at + jnp.where(line >= z * NB_SRC, height // parts - NB_SRC, 0)
+    listed = ones(at == iota((count, height), 1))
+    notes = jnp.dot(listed, packed, preferred_element_type=jnp.float32).astype(jnp.int32)
     left, right, owner, source = [notes[:, i : i + 1] for i in range(4)]
     across = iota((count, height), 1)
+    flip = place * blocks
     picks = []
     for block in (left, right):
         for offset in range(BLK * WINDOWS):
-            hit = across == block * (BLK * WINDOWS) + offset
-            picks.append(hit.astype(jnp.float32))
+            picks.append((across == jnp.bitwise_xor(block, flip) * (BLK * WINDOWS) + offset).astype(jnp.float32))
     rows_ref[...] = jnp.concatenate(picks, axis=0).astype(jnp.bfloat16)
 
     owned = (iota((count, LANES), 1) == owner).astype(jnp.float32)
     other = iota((count, count), 1)
-    before = jnp.logical_and(other < iota((count, count), 0), other >= source * NB_SRC)
-    before = before.astype(jnp.float32).astype(jnp.bfloat16)
+    before = ones(jnp.logical_and(other < iota((count, count), 0), other >= jnp.bitwise_xor(source, place) * NB_SRC))
     seen = jnp.dot(before, owned.astype(jnp.bfloat16), preferred_element_type=jnp.float32)
-    rank = jnp.sum(owned * seen, axis=1, keepdims=True)
+    rank = jnp.sum(owned * seen, axis=1, keepdims=True).astype(jnp.int32)
     target = ((owner * parts + source) * MOST + rank) * PAIRS
     across = iota((count, place_ref.shape[1]), 1)
     places = [(across == target + n).astype(jnp.float32) for n in range(PAIRS)]
     place_ref[...] = jnp.concatenate(places, axis=0).astype(jnp.bfloat16)
 
 
-def corr_kernel(per_step, parts, notes_ref, panel_ref, table_ref, out_ref, total, rows_ref, place_ref):
+def corr_kernel(per_step, parts, place, *refs):
+    note_refs, panel_refs = refs[:parts], refs[parts : 2 * parts]
+    table_ref, out_ref, total, rows_ref, place_ref = refs[2 * parts :]
     step = pl.program_id(0)
     count = total.shape[0] // PAIRS
 
     @pl.when(step == 0)
     def prepare():
-        choosers(parts, notes_ref, rows_ref, place_ref)
-
-    chosen = jnp.dot(rows_ref[...], panel_ref[...], preferred_element_type=jnp.float32)
+        choosers(parts, place[0], jnp.concatenate([ref[...] for ref in note_refs]), rows_ref, place_ref)
+
+    panel = jnp.concatenate([ref[...] for ref in panel_refs])
+    chosen = jnp.dot(rows_ref[...], panel, preferred_element_type=jnp.float32)
 
     def row(side, channel, window, start):
         first = ((side * BLK + channel) * WINDOWS + window) * count
@@ -195,27 +207,29 @@
         ).astype(jnp.bfloat16)
 
 
-def correlate(panel, table, groups, parts):
+def correlate(panels, table, place, groups):
     per_step = 4
+    parts = len(panels)
     span = per_step * 2 * LANES
-    height = panel.shape[0]
-    steps = panel.shape[1] // span
+    deep = panels[0].shape[0]
+    steps = panels[0].shape[1] // span
     pairs = parts * NB_SRC * PAIRS
     slots = groups * parts * MOST * PAIRS
     return pl.pallas_call(
         functools.partial(corr_kernel, per_step, parts),
-        grid=(steps,),
-        in_specs=[
-            pl.BlockSpec((height, LANES), lambda i: (0, steps * span // LANES)),
-            pl.BlockSpec((height, span), lambda i: (0, i)),
-            pl.BlockSpec((span, LAGS), lambda i: (i, 0)),
-        ],
-        out_specs=pl.BlockSpec((slots, LAGS), lambda i: (0, 0)),
-        scratch_shapes=[
-            pltpu.VMEM((pairs, LAGS), jnp.float32),
-            pltpu.VMEM((2 * pairs, height), jnp.bfloat16),
-            pltpu.VMEM((pairs, slots), jnp.bfloat16),
-        ],
+        grid_spec=pltpu.PrefetchScalarGridSpec(
+            num_scalar_prefetch=1,
+            grid=(steps,),
+            in_specs=[pl.BlockSpec((deep, LANES), lambda i, place: (0, steps * span // LANES))] * parts
+            + [pl.BlockSpec((deep, span), lambda i, place: (0, i))] * parts
+            + [pl.BlockSpec((span, LAGS), lambda i, place: (i, 0))],
+            out_specs=pl.BlockSpec((slots, LAGS), lambda i, place: (0, 0)),
+            scratch_shapes=[
+                pltpu.VMEM((pairs, LAGS), jnp.float32),
+                pltpu.VMEM((2 * pairs, deep * parts), jnp.bfloat16),
+                pltpu.VMEM((pairs, slots), jnp.bfloat16),
+            ],
+        ),
         out_shape=jax.ShapeDtypeStruct((slots, LAGS), jnp.bfloat16),
         compiler_params=pltpu.CompilerParams(vmem_limit_bytes=VMEM_LIMIT),
         cost_estimate=pl.CostEstimate(
@@ -224,7 +238,7 @@
             transcendentals=0,
         ),
         name="correlate",
-    )(panel, panel, table)
+    )(place[None], *panels, *panels, table)
 
 
 def local(spectra, pair_blocks, owners):
@@ -239,12 +253,12 @@
     notes = jnp.where(lane == 0, blocks[:, :1], jnp.where(lane == 1, blocks[:, 1:], place))
     notes = jnp.where(lane == 2, owners[0, 0], notes).astype(jnp.bfloat16)
     notes = jnp.pad(notes, ((0, rows - NB_SRC), (0, 0)))
-    white = whiten(spectra, notes, parts)
-    panel = lax.all_to_all(white, "chan", split_axis=0, concat_axis=0, tiled=True)
-    panel = panel.reshape(parts * rows, white.shape[2])
+    panels = list(whiten(spectra, notes, place, parts))
+    for d in reversed(range(1, parts)):
+        panels[d] = lax.ppermute(panels[d], "chan", [(i, i ^ d) for i in range(parts)])
 
     table = tables(place, chunks)
-    corr = correlate(panel, table, groups, parts)
+    corr = correlate(panels, table, place, groups)
     corr = corr.reshape(groups * parts, MOST, PAIRS, LAGS)
     got = lax.all_to_all(corr, ("grp", "chan"), split_axis=0, concat_axis=0, tiled=True)
     got = got.reshape(groups, parts, MOST, PAIRS, LAGS).astype(jnp.float32)

time: 74 us -> 71.8 us (0.970)
  waiting for transfers between devices: 13.3 us -> 6.36 us
  blocking collectives: 23.1 us -> 27.6 us
    all_to_all x1 -> x0, waiting for transfers between devices: 13.3 us -> none  [local(): lax.all_to_all(white, 'chan', split_axis=0, concat_axis=0, tiled=True)]
    ppermute x0 -> x3, waiting for transfers between devices: none -> 6.36 us  [local(): lax.ppermute(panels[d], 'chan', [(i, i ^ d) for i in range(parts)])]
    all_to_all x1 -> x0, starting transfers between devices: 6.33 us -> none  [local(): lax.all_to_all(white, 'chan', split_axis=0, concat_axis=0, tiled=True)]
    ppermute x0 -> x3, starting transfers between devices: none -> 5.65 us  [local(): lax.ppermute(panels[d], 'chan', [(i, i ^ d) for i in range(parts)])]
    all_to_all x1, blocking collectives: 23.1 us -> 27.6 us  [local(): lax.all_to_all(corr, ('grp', 'chan'), split_axis=0, concat_axis=0, tiled=...]
  transfers between devices with their start and end apart: 1 -> 3, of which waited for: 1 -> 1; matrix products, arithmetic and copies ran while one was open for 5% -> 6% of each run, Pallas kernels for 13% -> 13%
where the time goes in v1:
time: 71.8 us; the launch traced here: 70.5 us
  blocking collectives  27.6 us (38%)
  Pallas kernels  20.7 us (29%)
  waiting for transfers between devices  6.36 us (9%)
  other arithmetic  5.75 us (8%)
  starting transfers between devices  5.65 us (8%)
  local copies, waits for them, and re-layouts  4.43 us (6%)
    all_to_all x1, blocking collectives, local(): lax.all_to_all(corr, ('grp', 'chan'), split_axis=0, concat_axis=0, tiled=...  27.6 us
    pallas_call x1, Pallas kernels, tables(): pl.pallas_call(table_kernel, grid_spec=pltpu.PrefetchScalarGridSpec(num_s...  9.25 us
    pallas_call x1, Pallas kernels, correlate(): pl.pallas_call(functools.partial(corr_kernel, per_step, parts), grid_spec...  9.01 us
    ppermute x3, waiting for transfers between devices, local(): lax.ppermute(panels[d], 'chan', [(i, i ^ d) for i in range(parts)])  6.36 us
    ppermute x3, starting transfers between devices, local(): lax.ppermute(panels[d], 'chan', [(i, i ^ d) for i in range(parts)])  5.65 us
    sin x1, other arithmetic, tables(): jnp.sin(low)  2.9 us
    reshape x1, local copies, waits for them, and re-layouts, whiten(): planes = jnp.transpose(spectra.reshape(rows, 2, F), (1, 0, 2))  2.78 us
    pallas_call x1, Pallas kernels, whiten(): pl.pallas_call(functools.partial(whiten_kernel, parts), grid_spec=pltpu.P...  2.39 us
  transfers between devices with their start and end apart: 3, of which 1 were waited for; matrix products, arithmetic and copies ran while one was open for 6% of the time, Pallas kernels for 13%

profile of v1, /device:TPU:0, one launch (start us, length us, event | category | flops | bytes accessed | tf_op | source)
XLA Modules:
  0.0 70.5 jit_solution(12814680126526245572)
XLA Ops:
  0.0 0.8 %slice_bitcast_fusion.1 = (s32[18]{0:T(128)S(1)}, s32[18]{0:T(128)S(1)}) fusion(s32[18,2]{0,1:T(2,128)} %bitcast.17), kind=kLoop, calls=%fused_computation.28 | loop fusion | bytes 288 | tf_op jit(solution)/shard_map/jit(_where)/broadcast_in_dim | solution.py:253
  0.8 2.8 %copy.7 = bf16[32,2,8192]{2,0,1:T(8,128)(2,1)} copy(bf16[32,2,8192]{2,1,0:T(2,128)(2,1)} %bitcast.16) | data formatting | bytes 2097152 | tf_op jit(solution)/shard_map/reshape | solution.py:53
  3.5 0.7 %select_convert_fusion = bf16[18,128]{1,0:T(8,128)(2,1)S(1)} fusion(s32[]{:T(128)} %axis_index.12, s32[18]{0:T(128)S(1)} %get-tuple-element.18, s32[18]{0:T(128)S(1)} %get-tuple-element.17, s32[18]{0:T(128)} %bitcast.18, pred[128]{0:T(512)(128)(4,1)S(1)} %get-tuple-element.19, pred[128]{0:T(512)(128)(4,1)S(1)} %get-tuple-element.20, ...), kind=kLoop, calls=%fused_computation.23 | loop fusion | flops 9216 | bytes 5212 | tf_op jit(solution)/shard_map/convert_element_type | solution.py:254
  4.3 0.6 pad.4.notes_ref
  4.9 2.4 %whiten.1 = (bf16[32,4224]{1,0:T(8,128)(2,1)}, bf16[32,4224]{1,0:T(8,128)(2,1)}, bf16[32,4224]{1,0:T(8,128)(2,1)}, bf16[32,4224]{1,0:T(8,128)(2,1)}) custom-call(s32[1]{0:T(128)} %bitcast.place_ref.first_ref.place, bf16[2,32,8192]{2,1,0:T(8,128)(2,1)} %bitcast.15, bf16[32,128]{1,0:T(8,128)(2,1)} %pad.4.notes_ref), custom_call_target="tpu_custom_call" | custom-call | tf_op jit(solution)/shard_map/whiten/pallas_call | solution.py:55
  7.3 0.0 copy-start
  7.3 3.1 %collective-permute-start = (bf16[32,4224]{1,0:T(8,128)(2,1)}, bf16[32,4224]{1,0:T(8,128)(2,1)S(1)}, u32[]{:S(2)}, u32[]{:S(2)}) collective-permute-start(bf16[32,4224]{1,0:T(8,128)(2,1)} %get-tuple-element.10), channel_id=1, source_target_pairs={{0,1},{1,0},{2,3},{3,2},{4,5},{5,4},{6,7},{7,6},{8,9},{9,8},{10,11... | collective-permute-start | bytes 811016 | tf_op jit(solution)/shard_map/ppermute | solution.py:258
  10.3 2.6 %collective-permute-start.1 = (bf16[32,4224]{1,0:T(8,128)(2,1)}, bf16[32,4224]{1,0:T(8,128)(2,1)S(1)}, u32[]{:S(2)}, u32[]{:S(2)}) collective-permute-start(bf16[32,4224]{1,0:T(8,128)(2,1)} %get-tuple-element.11), channel_id=1, source_target_pairs={{0,2},{1,3},{2,0},{3,1},{4,6},{5,7},{6,4},{7,5},{8,10},{9,11},{10,... | collective-permute-start | bytes 811016 | tf_op jit(solution)/shard_map/ppermute | solution.py:258
  12.9 0.0 collective-permute-start.2
  12.9 1.0 %sine_multiply_fusion = (f32[16,1024]{1,0:T(8,128)}, f32[16,1024]{1,0:T(8,128)}) fusion(s32[1024]{0:T(1024)S(1)} %iota_add_fusion, s32[16]{0:T(128)S(1)} %add_multiply_fusion), kind=kLoop, calls=%fused_computation.21 | loop fusion | flops 262144 | bytes 135232 | tf_op jit(solution)/shard_map/mul | solution.py:113
  13.9 2.9 %fusion.6 = (f32[128,1024]{1,0:T(8,128)}, f32[128,1024]{1,0:T(8,128)}) fusion(s32[1024]{0:T(1024)S(1)} %iota_add_fusion), kind=kLoop, calls=%fused_computation.11 | loop fusion | flops 1835008 | bytes 1052672 | tf_op jit(solution)/shard_map/sin | solution.py:113
  16.8 9.3 %tables.1.refs_8_ = bf16[4096,1024]{1,0:T(8,128)(2,1)} custom-call(s32[1]{0:T(128)} %bitcast.place_ref.first_ref.place, f32[16,1024]{1,0:T(8,128)} %get-tuple-element.14.hi_cos_ref, f32[16,1024]{1,0:T(8,128)} %get-tuple-element.13.hi_sin_ref, f32[128,1024]{1,0:T(8,128)} %get-tuple-element.16.lo_cos_ref, f32[128,1024]{1,0:T(8,128)} %get-tuple-element.15.lo_sin_ref), custom_call_target="tpu_custom_call" | custom-call | flops 16777216 | bytes 8388608 | tf_op jit(solution)/shard_map/tables/pallas_call | solution.py:95
  26.1 0.0 collective-permute-done.refs_1_.refs_5_
  26.1 6.4 %collective-permute-done.1.refs_2_.refs_6_ = bf16[32,4224]{1,0:T(8,128)(2,1)S(1)} collective-permute-done((bf16[32,4224]{1,0:T(8,128)(2,1)}, bf16[32,4224]{1,0:T(8,128)(2,1)S(1)}, u32[]{:S(2)}, u32[]{:S(2)}) %collective-permute-start.1) | collective-permute-done | bytes 270368 | tf_op jit(solution)/shard_map/ppermute | solution.py:258
  32.4 0.0 collective-permute-done.2.refs_3_.refs_7_
  32.5 0.0 copy-done
  32.5 9.0 %correlate.1 = bf16[384,1024]{1,0:T(8,128)(2,1)S(1)} custom-call(s32[1]{0:T(128)} %bitcast.place_ref.first_ref.place, bf16[32,4224]{1,0:T(8,128)(2,1)S(1)} %copy-done, bf16[32,4224]{1,0:T(8,128)(2,1)S(1)} %collective-permute-done.refs_1_.refs_5_, bf16[32,4224]{1,0:T(8,128)(2,1)S(1)} %collective-permute-done.1.refs_2_.refs_6_, ...), custom_call_target="tpu_custom_call" | custom-call | flops 2415919104 | bytes 8388608 | tf_op jit(solution)/shard_map/correlate/pallas_call | solution.py:218
  41.5 0.3 reshape.23
  41.8 27.6 %all_to_all.5 = bf16[32,3,4,1024]{3,2,1,0:T(4,128)(2,1)S(1)} all-to-all(bf16[32,3,4,1024]{3,2,1,0:T(4,128)(2,1)S(1)} %reshape.23), channel_id=1, replica_groups=mesh['grp'=8,'chan'=4] {'grp','chan'}, dimensions={0} | all-to-all | bytes 1572864 | tf_op jit(solution)/shard_map/all_to_all | solution.py:263
  69.4 1.1 %convert_reduce_fusion = f32[8,3,4,1024]{3,2,1,0:T(4,128)} fusion(bf16[32,3,4,1024]{3,2,1,0:T(4,128)(2,1)S(1)} %all_to_all.5), kind=kLoop, calls=%fused_computation | loop fusion | flops 688128 | bytes 1179648 | tf_op jit(solution)/shard_map/reduce_sum | solution.py:265
  (4 shorter events, 0.0 us)
Async XLA Ops:
  7.3 25.2 %copy-start = (bf16[32,4224]{1,0:T(8,128)(2,1)S(1)}, bf16[32,4224]{1,0:T(8,128)(2,1)}, u32[]{:S(2)}) copy-start(bf16[32,4224]{1,0:T(8,128)(2,1)} %get-tuple-element.9.refs_0_.refs_4_) | copy-start | bytes 811012
  7.3 18.8 %collective-permute-start = (bf16[32,4224]{1,0:T(8,128)(2,1)}, bf16[32,4224]{1,0:T(8,128)(2,1)S(1)}, u32[]{:S(2)}, u32[]{:S(2)}) collective-permute-start(bf16[32,4224]{1,0:T(8,128)(2,1)} %get-tuple-element.10), channel_id=1, source_target_pairs={{0,1},{1,0},{2,3},{3,2},{4,5},{5,4},{6,7},{7,6},{8,9},{9,8},{10,11... | collective-permute-start | bytes 811016 | tf_op jit(solution)/shard_map/ppermute | solution.py:258
  10.3 22.1 %collective-permute-start.1 = (bf16[32,4224]{1,0:T(8,128)(2,1)}, bf16[32,4224]{1,0:T(8,128)(2,1)S(1)}, u32[]{:S(2)}, u32[]{:S(2)}) collective-permute-start(bf16[32,4224]{1,0:T(8,128)(2,1)} %get-tuple-element.11), channel_id=1, source_target_pairs={{0,2},{1,3},{2,0},{3,1},{4,6},{5,7},{6,4},{7,5},{8,10},{9,11},{10,... | collective-permute-start | bytes 811016 | tf_op jit(solution)/shard_map/ppermute | solution.py:258
  12.9 19.5 %collective-permute-start.2 = (bf16[32,4224]{1,0:T(8,128)(2,1)}, bf16[32,4224]{1,0:T(8,128)(2,1)S(1)}, u32[]{:S(2)}, u32[]{:S(2)}) collective-permute-start(bf16[32,4224]{1,0:T(8,128)(2,1)} %get-tuple-element.12), channel_id=1, source_target_pairs={{0,3},{1,2},{2,1},{3,0},{4,7},{5,6},{6,5},{7,4},{8,11},{9,10},{10,... | collective-permute-start | bytes 811016 | tf_op jit(solution)/shard_map/ppermute | solution.py:258

commit v2 on v1

--- a/solution.py
+++ b/solution.py
@@ -16,12 +16,15 @@
 LANES = 128
 PAIRS = BLK * BLK
 VMEM_LIMIT = 48 * 1024 * 1024
-
-
-def whiten_kernel(parts, place_ref, spec_ref, notes_ref, *out_refs):
+HALVES = 2
+JOINT = 1
+
+
+def whiten_kernel(parts, second, place_ref, spec_ref, *refs):
     blocks = F // LANES
     each = blocks // parts
     place = place_ref[0]
+    out_refs = list(refs[-parts:])
 
     def values(start):
         span = pl.ds(start, LANES)
@@ -29,8 +32,23 @@
         im = spec_ref[1, :, span].astype(jnp.float32)
         return re, im, re * re + im * im
 
-    for out_ref in out_refs:
-        out_ref[:, each * 2 * LANES :] = notes_ref[...]
+    if second:
+        deep = spec_ref.shape[1]
+        joint = out_refs[JOINT]
+        joint[:deep] = refs[0][...]
+        joint[deep:, each * 2 * LANES :] = jnp.zeros((deep, LANES), jnp.bfloat16)
+        out_refs[JOINT] = joint.at[deep:]
+    else:
+        pairs_ref, owners_ref = refs[:2]
+        shape = (spec_ref.shape[1], LANES)
+        line = lax.broadcasted_iota(jnp.int32, shape, 0)
+        spare = jnp.zeros((1, LANES - NB_SRC), jnp.int32)
+        wide = lambda row: jnp.broadcast_to(jnp.concatenate([row, spare], axis=1), shape)
+        notes = jnp.where(line == 0, wide(pairs_ref[0:1]), jnp.where(line == 1, wide(pairs_ref[1:2]), place))
+        notes = jnp.where(line == 2, wide(owners_ref[...]), notes)
+        notes = notes.astype(jnp.float32).astype(jnp.bfloat16)
+        for out_ref in out_refs:
+            out_ref[:, each * 2 * LANES :] = notes
     sums = [None] * 4
     for k in range(blocks):
         power = values(k * LANES)[2]
@@ -47,25 +65,25 @@
             out_ref[:, at + LANES : at + 2 * LANES] = (im * scale).astype(jnp.bfloat16)
 
 
-def whiten(spectra, notes, place, parts):
+def whiten(spectra, others, place, parts, second):
     rows = spectra.shape[0] * WINDOWS
-    step = 16
     planes = jnp.transpose(spectra.reshape(rows, 2, F), (1, 0, 2))
-    width = 2 * F // parts + LANES
-    return pl.pallas_call(
-        functools.partial(whiten_kernel, parts),
+    width = 2 * F // parts
+    shapes = [(rows, width if second else width + LANES)] * parts
+    if second:
+        shapes[JOINT] = (HALVES * rows, width + LANES)
+    whole = lambda array: pl.BlockSpec(array.shape, lambda i, place: (0,) * array.ndim)
+    return list(pl.pallas_call(
+        functools.partial(whiten_kernel, parts, second),
         grid_spec=pltpu.PrefetchScalarGridSpec(
             num_scalar_prefetch=1,
-            grid=(rows // step,),
-            in_specs=[
-                pl.BlockSpec((2, step, F), lambda i, place: (0, i, 0)),
-                pl.BlockSpec((step, LANES), lambda i, place: (i, 0)),
-            ],
-            out_specs=[pl.BlockSpec((step, width), lambda i, place: (i, 0))] * parts,
-        ),
-        out_shape=[jax.ShapeDtypeStruct((rows, width), jnp.bfloat16)] * parts,
+            grid=(1,),
+            in_specs=[whole(array) for array in [planes, *others]],
+            out_specs=[pl.BlockSpec(shape, lambda i, place: (0, 0)) for shape in shapes],
+        ),
+        out_shape=[jax.ShapeDtypeStruct(shape, jnp.bfloat16) for shape in shapes],
         name="whiten",
-    )(place[None], planes, notes)
+    )(place[None], planes, *others))
 
 
 def table_kernel(first_ref, hi_cos_ref, hi_sin_ref, lo_cos_ref, lo_sin_ref, out_ref):
@@ -115,8 +133,8 @@
 
 def choosers(parts, place, packed, rows_ref, place_ref):
     count = parts * NB_SRC
-    height = packed.shape[0]
-    blocks = height // parts // (BLK * WINDOWS)
+    height = rows_ref.shape[1]
+    blocks = packed.shape[0] // parts // (BLK * WINDOWS)
 
     def iota(shape, axis):
         return lax.broadcasted_iota(jnp.int32, shape, axis)
@@ -124,19 +142,28 @@
     def ones(hit):
         return hit.astype(jnp.float32).astype(jnp.bfloat16)
 
-    line = iota((count, height), 0)
-    at = line
+    line = iota((count, 1), 0)
+    group = jnp.zeros_like(line)
     for z in range(1, parts):
-        at = at + jnp.where(line >= z * NB_SRC, height // parts - NB_SRC, 0)
-    listed = ones(at == iota((count, height), 1))
-    notes = jnp.dot(listed, packed, preferred_element_type=jnp.float32).astype(jnp.int32)
-    left, right, owner, source = [notes[:, i : i + 1] for i in range(4)]
+        group = group + jnp.where(line >= z * NB_SRC, 1, 0)
+    deep = packed.shape[0] // parts
+    here = iota((count, LANES), 1) == line - group * NB_SRC
+
+    def column(kind):
+        row = ones(iota((count, packed.shape[0]), 1) == group * deep + kind)
+        found = jnp.dot(row, packed, preferred_element_type=jnp.float32)
+        return jnp.sum(jnp.where(here, found, 0.0), axis=1, keepdims=True).astype(jnp.int32)
+
+    left, right, owner, source = [column(kind) for kind in range(4)]
     across = iota((count, height), 1)
-    flip = place * blocks
     picks = []
     for block in (left, right):
+        place_of = jnp.bitwise_xor(lax.shift_right_logical(block, (HALVES * blocks).bit_length() - 1), place)
+        half = jnp.bitwise_and(lax.shift_right_logical(block, blocks.bit_length() - 1), HALVES - 1)
+        inner = jnp.bitwise_and(block, blocks - 1)
+        first = (half * parts + place_of) * deep + inner * (BLK * WINDOWS)
         for offset in range(BLK * WINDOWS):
-            picks.append((across == jnp.bitwise_xor(block, flip) * (BLK * WINDOWS) + offset).astype(jnp.float32))
+            picks.append((across == first + offset).astype(jnp.float32))
     rows_ref[...] = jnp.concatenate(picks, axis=0).astype(jnp.bfloat16)
 
     owned = (iota((count, LANES), 1) == owner).astype(jnp.float32)
@@ -151,14 +178,17 @@
 
 
 def corr_kernel(per_step, parts, place, *refs):
-    note_refs, panel_refs = refs[:parts], refs[parts : 2 * parts]
-    table_ref, out_ref, total, rows_ref, place_ref = refs[2 * parts :]
+    note_refs, panel_refs = refs[:parts], list(refs[parts : 3 * parts - 1])
+    table_ref, out_ref, total, rows_ref, place_ref = refs[3 * parts - 1 :]
+    deep = panel_refs[0].shape[0]
+    panel_refs.insert(parts + JOINT, panel_refs[JOINT].at[deep:])
+    panel_refs[JOINT] = panel_refs[JOINT].at[:deep]
     step = pl.program_id(0)
     count = total.shape[0] // PAIRS
 
     @pl.when(step == 0)
     def prepare():
-        choosers(parts, place[0], jnp.concatenate([ref[...] for ref in note_refs]), rows_ref, place_ref)
+        choosers(parts, place[0], jnp.concatenate([ref[:deep] for ref in note_refs]), rows_ref, place_ref)
 
     panel = jnp.concatenate([ref[...] for ref in panel_refs])
     chosen = jnp.dot(rows_ref[...], panel, preferred_element_type=jnp.float32)
@@ -207,12 +237,11 @@
         ).astype(jnp.bfloat16)
 
 
-def correlate(panels, table, place, groups):
+def correlate(panels, table, place, groups, parts):
     per_step = 4
-    parts = len(panels)
     span = per_step * 2 * LANES
     deep = panels[0].shape[0]
-    steps = panels[0].shape[1] // span
+    steps = table.shape[0] // span
     pairs = parts * NB_SRC * PAIRS
     slots = groups * parts * MOST * PAIRS
     return pl.pallas_call(
@@ -220,13 +249,16 @@
         grid_spec=pltpu.PrefetchScalarGridSpec(
             num_scalar_prefetch=1,
             grid=(steps,),
-            in_specs=[pl.BlockSpec((deep, LANES), lambda i, place: (0, steps * span // LANES))] * parts
-            + [pl.BlockSpec((deep, span), lambda i, place: (0, i))] * parts
+            in_specs=[
+                pl.BlockSpec((array.shape[0], LANES), lambda i, place: (0, steps * span // LANES))
+                for array in panels[:parts]
+            ]
+            + [pl.BlockSpec((array.shape[0], span), lambda i, place: (0, i)) for array in panels]
             + [pl.BlockSpec((span, LAGS), lambda i, place: (i, 0))],
             out_specs=pl.BlockSpec((slots, LAGS), lambda i, place: (0, 0)),
             scratch_shapes=[
                 pltpu.VMEM((pairs, LAGS), jnp.float32),
-                pltpu.VMEM((2 * pairs, deep * parts), jnp.bfloat16),
+                pltpu.VMEM((2 * pairs, deep * parts * HALVES), jnp.bfloat16),
                 pltpu.VMEM((pairs, slots), jnp.bfloat16),
             ],
         ),
@@ -238,7 +270,7 @@
             transcendentals=0,
         ),
         name="correlate",
-    )(place[None], *panels, *panels, table)
+    )(place[None], *panels[:parts], *panels, table)
 
 
 def local(spectra, pair_blocks, owners):
@@ -246,19 +278,24 @@
     parts = lax.axis_size("chan")
     place = lax.axis_index("chan")
     chunks = F // LANES // parts
-    rows = spectra.shape[0] * WINDOWS
-
-    lane = lax.broadcasted_iota(jnp.int32, (NB_SRC, LANES), 1)
-    blocks = pair_blocks[0, 0]
-    notes = jnp.where(lane == 0, blocks[:, :1], jnp.where(lane == 1, blocks[:, 1:], place))
-    notes = jnp.where(lane == 2, owners[0, 0], notes).astype(jnp.bfloat16)
-    notes = jnp.pad(notes, ((0, rows - NB_SRC), (0, 0)))
-    panels = list(whiten(spectra, notes, place, parts))
-    for d in reversed(range(1, parts)):
-        panels[d] = lax.ppermute(panels[d], "chan", [(i, i ^ d) for i in range(parts)])
+    lists = [pair_blocks[0, 0].T, owners[0, 0].T]
+    each = spectra.shape[0] // HALVES
+    def swap(array, d):
+        return lax.ppermute(array, "chan", [(i, i ^ d) for i in range(parts)])
+
+    first = whiten(spectra[:each], lists, place, parts, False)
+    apart = [d for d in reversed(range(1, parts)) if d != JOINT]
+    spectra, ready = lax.optimization_barrier((spectra, first[JOINT]))
+    for d in apart:
+        first[d] = swap(first[d], d)
+    second = whiten(spectra[each:], [ready], place, parts, True)
+    for d in apart:
+        second[d] = swap(second[d], d)
+    first[JOINT] = swap(second.pop(JOINT), JOINT)
+    panels = first + second
 
     table = tables(place, chunks)
-    corr = correlate(panels, table, place, groups)
+    corr = correlate(panels, table, place, groups, parts)
     corr = corr.reshape(groups * parts, MOST, PAIRS, LAGS)
     got = lax.all_to_all(corr, ("grp", "chan"), split_axis=0, concat_axis=0, tiled=True)
     got = got.reshape(groups, parts, MOST, PAIRS, LAGS).astype(jnp.float32)

time: 71.8 us -> 68.6 us (0.955)
  waiting for transfers between devices: 6.36 us -> 0.01 us
  starting transfers between devices: 5.65 us -> 8.87 us
  blocking collectives: 27.6 us -> 25.4 us
  Pallas kernels: 20.7 us -> 22.5 us
  local copies, waits for them, and re-layouts: 4.43 us -> 5.34 us
  other arithmetic: 5.75 us -> 5.03 us
    ppermute x3 -> x5, waiting for transfers between devices: 6.36 us -> 0.01 us  [swap(): return lax.ppermute(array, 'chan', [(i, i ^ d) for i in range(parts)])]
    ppermute x3 -> x5, starting transfers between devices: 5.65 us -> 8.87 us  [swap(): return lax.ppermute(array, 'chan', [(i, i ^ d) for i in range(parts)])]
    slice x0 -> x2, local copies, waits for them, and re-layouts: none -> 2.85 us  [the longest x1 1.43 us: local(): first = whiten(spectra[:each], lists, place, parts, False)]
    all_to_all x1, blocking collectives: 27.6 us -> 25.4 us  [local(): lax.all_to_all(corr, ('grp', 'chan'), split_axis=0, concat_axis=0, tiled=...]
    pallas_call x1 -> x2, Pallas kernels: 2.39 us -> 4.16 us  [whiten(): pl.pallas_call(functools.partial(whiten_kernel, parts, second), grid_spec...]
    broadcast_in_dim x1 -> x0, local copies, waits for them, and re-layouts: 0.76 us -> none  [local(): jnp.where(lane == 0, blocks[:, :1], jnp.where(lane == 1, blocks[:, 1:], p...]
    convert_element_type x1 -> x0, other arithmetic: 0.73 us -> none  [local(): notes = jnp.where(lane == 2, owners[0, 0], notes).astype(jnp.bfloat16)]
    reshape x1 -> x2, local copies, waits for them, and re-layouts: 2.78 us -> 2.19 us  [whiten(): planes = jnp.transpose(spectra.reshape(rows, 2, F), (1, 0, 2))]
  transfers between devices with their start and end apart: 3 -> 5, of which waited for: 1 -> 0; matrix products, arithmetic and copies ran while one was open for 6% -> 10% of each run, Pallas kernels for 13% -> 17%
where the time goes in v2:
time: 68.6 us; the launch traced here: 67.2 us
  blocking collectives  25.4 us (37%)
  Pallas kernels  22.5 us (33%)
  starting transfers between devices  8.87 us (13%)
  local copies, waits for them, and re-layouts  5.34 us (8%)
  other arithmetic  5.03 us (7%)
    all_to_all x1, blocking collectives, local(): lax.all_to_all(corr, ('grp', 'chan'), split_axis=0, concat_axis=0, tiled=...  25.4 us
    pallas_call x1, Pallas kernels, tables(): pl.pallas_call(table_kernel, grid_spec=pltpu.PrefetchScalarGridSpec(num_s...  9.28 us
    pallas_call x1, Pallas kernels, correlate(): pl.pallas_call(functools.partial(corr_kernel, per_step, parts), grid_spec...  9.07 us
    ppermute x5, starting transfers between devices, swap(): return lax.ppermute(array, 'chan', [(i, i ^ d) for i in range(parts)])  8.87 us
    pallas_call x2, Pallas kernels, whiten(): pl.pallas_call(functools.partial(whiten_kernel, parts, second), grid_spec...  4.16 us
    sin x1, other arithmetic, tables(): jnp.sin(low)  2.91 us
    reshape x2, local copies, waits for them, and re-layouts, whiten(): planes = jnp.transpose(spectra.reshape(rows, 2, F), (1, 0, 2))  2.19 us
    slice x1, local copies, waits for them, and re-layouts, local(): first = whiten(spectra[:each], lists, place, parts, False)  1.43 us
  transfers between devices with their start and end apart: 5, of which 0 were waited for; matrix products, arithmetic and copies ran while one was open for 10% of the time, Pallas kernels for 17%

profile of v2, /device:TPU:0, one launch (start us, length us, event | category | flops | bytes accessed | tf_op | source)
XLA Modules:
  0.0 67.2 jit_solution(6042875014817022102)
XLA Ops:
  0.0 1.4 %slice.6 = bf16[8,2,2,8192]{3,2,1,0:T(2,128)(2,1)S(1)} slice(bf16[16,2,2,8192]{3,2,1,0:T(2,128)(2,1)} %param.3), slice={[0:8], [0:2], [0:2], [0:8192]} | slice | bytes 1048576 | tf_op jit(solution)/shard_map/slice | solution.py:286
  1.4 1.1 %copy.11 = bf16[16,2,8192]{2,0,1:T(8,128)(2,1)} copy(bf16[16,2,8192]{2,1,0:T(2,128)(2,1)S(1)} %bitcast.19) | data formatting | bytes 1048576 | tf_op jit(solution)/shard_map/reshape | solution.py:70
  2.5 2.1 %whiten.2 = (bf16[16,4224]{1,0:T(8,128)(2,1)}, bf16[16,4224]{1,0:T(8,128)(2,1)}, bf16[16,4224]{1,0:T(8,128)(2,1)}, bf16[16,4224]{1,0:T(8,128)(2,1)}) custom-call(s32[1]{0:T(128)} %bitcast.place_ref.first_ref.place, bf16[2,16,8192]{2,1,0:T(8,128)(2,1)} %bitcast.18, s32[2,18]{1,0:T(2,128)} %bitcast.21, s32[1,18]{1,0:T(1,128)} %bitcast.22), custom_call_target="tpu_custom_call" | custom-call | tf_op jit(solution)/shard_map/whiten/pallas_call | solution.py:76
  4.6 4.0 %collective-permute-start.1 = (bf16[16,4224]{1,0:T(8,128)(2,1)}, bf16[16,4224]{1,0:T(8,128)(2,1)S(1)}, u32[]{:S(2)}, u32[]{:S(2)}) collective-permute-start(bf16[16,4224]{1,0:T(8,128)(2,1)} %get-tuple-element.20), channel_id=1, source_target_pairs={{0,2},{1,3},{2,0},{3,1},{4,6},{5,7},{6,4},{7,5},{8,10},{9,11},{10,... | collective-permute-start | bytes 405512 | tf_op jit(solution)/shard_map/ppermute | solution.py:284
  8.6 1.3 %collective-permute-start.2 = (bf16[16,4224]{1,0:T(8,128)(2,1)}, bf16[16,4224]{1,0:T(8,128)(2,1)S(1)}, u32[]{:S(2)}, u32[]{:S(2)}) collective-permute-start(bf16[16,4224]{1,0:T(8,128)(2,1)} %get-tuple-element.21), channel_id=1, source_target_pairs={{0,3},{1,2},{2,1},{3,0},{4,7},{5,6},{6,5},{7,4},{8,11},{9,10},{10,... | collective-permute-start | bytes 405512 | tf_op jit(solution)/shard_map/ppermute | solution.py:284
  10.0 1.4 %slice.7 = bf16[8,2,2,8192]{3,2,1,0:T(2,128)(2,1)S(1)} slice(bf16[16,2,2,8192]{3,2,1,0:T(2,128)(2,1)} %param.3), slice={[8:16], [0:2], [0:2], [0:8192]} | slice | bytes 1048576 | tf_op jit(solution)/shard_map/slice | solution.py:291
  11.4 1.1 %copy.10 = bf16[16,2,8192]{2,0,1:T(8,128)(2,1)} copy(bf16[16,2,8192]{2,1,0:T(2,128)(2,1)S(1)} %bitcast.20) | data formatting | bytes 1048576 | tf_op jit(solution)/shard_map/reshape | solution.py:70
  12.5 2.1 %whiten.3 = (bf16[16,4096]{1,0:T(8,128)(2,1)}, bf16[32,4224]{1,0:T(8,128)(2,1)}, bf16[16,4096]{1,0:T(8,128)(2,1)}, bf16[16,4096]{1,0:T(8,128)(2,1)}) custom-call(s32[1]{0:T(128)} %bitcast.place_ref.first_ref.place, bf16[2,16,8192]{2,1,0:T(8,128)(2,1)} %bitcast.17, bf16[16,4224]{1,0:T(8,128)(2,1)} %get-tuple-element.18.refs_0_), custom_call_target="tpu_custom_call" | custom-call | tf_op jit(solution)/shard_map/whiten/pallas_call | solution.py:76
  14.6 1.7 %collective-permute-start.3 = (bf16[16,4096]{1,0:T(8,128)(2,1)}, bf16[16,4096]{1,0:T(8,128)(2,1)S(1)}, u32[]{:S(2)}, u32[]{:S(2)}) collective-permute-start(bf16[16,4096]{1,0:T(8,128)(2,1)} %get-tuple-element.23), channel_id=1, source_target_pairs={{0,2},{1,3},{2,0},{3,1},{4,6},{5,7},{6,4},{7,5},{8,10},{9,11},{10,... | collective-permute-start | bytes 393224 | tf_op jit(solution)/shard_map/ppermute | solution.py:284
  16.3 0.9 %collective-permute-start.4 = (bf16[16,4096]{1,0:T(8,128)(2,1)}, bf16[16,4096]{1,0:T(8,128)(2,1)S(1)}, u32[]{:S(2)}, u32[]{:S(2)}) collective-permute-start(bf16[16,4096]{1,0:T(8,128)(2,1)} %get-tuple-element.24), channel_id=1, source_target_pairs={{0,3},{1,2},{2,1},{3,0},{4,7},{5,6},{6,5},{7,4},{8,11},{9,10},{10,... | collective-permute-start | bytes 393224 | tf_op jit(solution)/shard_map/ppermute | solution.py:284
  17.2 0.9 %collective-permute-start = (bf16[32,4224]{1,0:T(8,128)(2,1)}, bf16[32,4224]{1,0:T(8,128)(2,1)S(1)}, u32[]{:S(2)}, u32[]{:S(2)}) collective-permute-start(bf16[32,4224]{1,0:T(8,128)(2,1)} %get-tuple-element.19), channel_id=1, source_target_pairs={{0,1},{1,0},{2,3},{3,2},{4,5},{5,4},{6,7},{7,6},{8,9},{9,8},{10,11... | collective-permute-start | bytes 811016 | tf_op jit(solution)/shard_map/ppermute | solution.py:284
  18.1 2.9 %fusion.6 = (f32[128,1024]{1,0:T(8,128)}, f32[128,1024]{1,0:T(8,128)}) fusion(s32[1024]{0:T(1024)S(1)} %iota_add_fusion), kind=kLoop, calls=%fused_computation.12 | loop fusion | flops 1835008 | bytes 1052672 | tf_op jit(solution)/shard_map/sin | solution.py:131
  21.0 1.0 %sine_multiply_fusion = (f32[16,1024]{1,0:T(8,128)}, f32[16,1024]{1,0:T(8,128)}) fusion(s32[1024]{0:T(1024)S(1)} %iota_add_fusion, s32[16]{0:T(128)S(1)} %add_multiply_fusion), kind=kLoop, calls=%fused_computation.22 | loop fusion | flops 262144 | bytes 135232 | tf_op jit(solution)/shard_map/mul | solution.py:131
  22.0 9.3 %tables.1.refs_11_ = bf16[4096,1024]{1,0:T(8,128)(2,1)} custom-call(s32[1]{0:T(128)} %bitcast.place_ref.first_ref.place, f32[16,1024]{1,0:T(8,128)} %get-tuple-element.26.hi_cos_ref, f32[16,1024]{1,0:T(8,128)} %get-tuple-element.25.hi_sin_ref, f32[128,1024]{1,0:T(8,128)} %get-tuple-element.28.lo_cos_ref, f32[128,1024]{1,0:T(8,128)} %get-tuple-element.27.lo_sin_ref), custom_call_target="tpu_custom_call" | custom-call | flops 16777216 | bytes 8388608 | tf_op jit(solution)/shard_map/tables/pallas_call | solution.py:113
  31.3 0.0 collective-permute-done.3.refs_9_
  31.3 0.0 collective-permute-done.4.refs_10_
  31.3 0.0 collective-permute-done.1.refs_2_.refs_6_
  31.3 0.0 collective-permute-done.2.refs_3_.refs_7_
  31.3 0.0 collective-permute-done.refs_1_.refs_5_
  31.3 0.0 copy-done
  31.4 9.1 %correlate.1 = bf16[384,1024]{1,0:T(8,128)(2,1)S(1)} custom-call(s32[1]{0:T(128)} %bitcast.place_ref.first_ref.place, bf16[16,4224]{1,0:T(8,128)(2,1)S(1)} %copy-done, bf16[32,4224]{1,0:T(8,128)(2,1)S(1)} %collective-permute-done.refs_1_.refs_5_, bf16[16,4224]{1,0:T(8,128)(2,1)S(1)} %collective-permute-done.1.refs_2_.refs_6_, ...), custom_call_target="tpu_custom_call" | custom-call | flops 2415919104 | bytes 8388608 | tf_op jit(solution)/shard_map/correlate/pallas_call | solution.py:247
  40.4 0.3 reshape.26
  40.7 25.4 %all_to_all.5 = bf16[32,3,4,1024]{3,2,1,0:T(4,128)(2,1)S(1)} all-to-all(bf16[32,3,4,1024]{3,2,1,0:T(4,128)(2,1)S(1)} %reshape.26), channel_id=1, replica_groups=mesh['grp'=8,'chan'=4] {'grp','chan'}, dimensions={0} | all-to-all | bytes 1572864 | tf_op jit(solution)/shard_map/all_to_all | solution.py:300
  66.1 1.1 %convert_reduce_fusion = f32[8,3,4,1024]{3,2,1,0:T(4,128)} fusion(bf16[32,3,4,1024]{3,2,1,0:T(4,128)(2,1)S(1)} %all_to_all.5), kind=kLoop, calls=%fused_computation | loop fusion | flops 688128 | bytes 1179648 | tf_op jit(solution)/shard_map/reduce_sum | solution.py:302
  (5 shorter events, 0.0 us)
Async XLA Ops:
  4.6 26.8 %copy-start = (bf16[16,4224]{1,0:T(8,128)(2,1)S(1)}, bf16[16,4224]{1,0:T(8,128)(2,1)}, u32[]{:S(2)}) copy-start(bf16[16,4224]{1,0:T(8,128)(2,1)} %get-tuple-element.15.refs_0_.refs_4_) | copy-start | bytes 405508
  4.6 26.7 %collective-permute-start.1 = (bf16[16,4224]{1,0:T(8,128)(2,1)}, bf16[16,4224]{1,0:T(8,128)(2,1)S(1)}, u32[]{:S(2)}, u32[]{:S(2)}) collective-permute-start(bf16[16,4224]{1,0:T(8,128)(2,1)} %get-tuple-element.20), channel_id=1, source_target_pairs={{0,2},{1,3},{2,0},{3,1},{4,6},{5,7},{6,4},{7,5},{8,10},{9,11},{10,... | collective-permute-start | bytes 405512 | tf_op jit(solution)/shard_map/ppermute | solution.py:284
  8.6 22.7 %collective-permute-start.2 = (bf16[16,4224]{1,0:T(8,128)(2,1)}, bf16[16,4224]{1,0:T(8,128)(2,1)S(1)}, u32[]{:S(2)}, u32[]{:S(2)}) collective-permute-start(bf16[16,4224]{1,0:T(8,128)(2,1)} %get-tuple-element.21), channel_id=1, source_target_pairs={{0,3},{1,2},{2,1},{3,0},{4,7},{5,6},{6,5},{7,4},{8,11},{9,10},{10,... | collective-permute-start | bytes 405512 | tf_op jit(solution)/shard_map/ppermute | solution.py:284
  14.6 16.7 %copy-start.1 = (bf16[16,4096]{1,0:T(8,128)(2,1)S(1)}, bf16[16,4096]{1,0:T(8,128)(2,1)}, u32[]{:S(2)}) copy-start(bf16[16,4096]{1,0:T(8,128)(2,1)} %get-tuple-element.22.refs_8_) | copy-start | bytes 393220
  14.6 16.7 %collective-permute-start.3 = (bf16[16,4096]{1,0:T(8,128)(2,1)}, bf16[16,4096]{1,0:T(8,128)(2,1)S(1)}, u32[]{:S(2)}, u32[]{:S(2)}) collective-permute-start(bf16[16,4096]{1,0:T(8,128)(2,1)} %get-tuple-element.23), channel_id=1, source_target_pairs={{0,2},{1,3},{2,0},{3,1},{4,6},{5,7},{6,4},{7,5},{8,10},{9,11},{10,... | collective-permute-start | bytes 393224 | tf_op jit(solution)/shard_map/ppermute | solution.py:284
  16.3 15.0 %collective-permute-start.4 = (bf16[16,4096]{1,0:T(8,128)(2,1)}, bf16[16,4096]{1,0:T(8,128)(2,1)S(1)}, u32[]{:S(2)}, u32[]{:S(2)}) collective-permute-start(bf16[16,4096]{1,0:T(8,128)(2,1)} %get-tuple-element.24), channel_id=1, source_target_pairs={{0,3},{1,2},{2,1},{3,0},{4,7},{5,6},{6,5},{7,4},{8,11},{9,10},{10,... | collective-permute-start | bytes 393224 | tf_op jit(solution)/shard_map/ppermute | solution.py:284
  17.2 14.1 %collective-permute-start = (bf16[32,4224]{1,0:T(8,128)(2,1)}, bf16[32,4224]{1,0:T(8,128)(2,1)S(1)}, u32[]{:S(2)}, u32[]{:S(2)}) collective-permute-start(bf16[32,4224]{1,0:T(8,128)(2,1)} %get-tuple-element.19), channel_id=1, source_target_pairs={{0,1},{1,0},{2,3},{3,2},{4,5},{5,4},{6,7},{7,6},{8,9},{9,8},{10,11... | collective-permute-start | bytes 811016 | tf_op jit(solution)/shard_map/ppermute | solution.py:284
